TPU v7x, 32 devices: a whole 2x2x4 slice. The times are simulated.
32 devices in a mesh: grp: 2 (over x), row: 8 (over z, y), lag: 2 (over core).
Axes of the slice: x: 2, y: 2, z: 4, core: 2. Of those that a mesh axis runs over, the one named last changes fastest.
Arguments:
- history: bfloat16 [400, 2080], P('grp', 'lag'), parts along dimension 0, may hold values from -6 to 6
- kernel: bfloat16 [256, 200, 2048], P(('grp', 'row'), None, 'lag'), parts along dimension 0, may hold values from -0.009765625 to 0.009765625
- tile_rows: int32 [128, 16], P(('grp', 'row')), parts along dimension 0, may hold values from 0 to 15
- tile_counts: int32 [128], P(('grp', 'row')), parts along dimension 0, may hold values from 1 to 16
- owner: int32 [128, 1], P(('grp', 'row')), parts along dimension 0, may hold values from 0 to 7; in each aligned block of 8 rows (0 to 7, 8 to 15, ...) at most 2 rows name the same one
- spline: bfloat16 [128, 16, 128], P(('grp', 'row')), parts along dimension 0, may hold values from -0.5 to 0.5
- mode_shapes: float32 [2048, 200], P(('grp', 'row')), parts along dimension 0, may hold values from -0.1875 to 0.1875
Outputs:
- nodal_forces: float32 [32, 2048], P('lag', ('grp', 'row')), parts along dimension 1
- modal_forces: float32 [32, 400], P('lag', 'grp'), parts along dimension 1
There are 2 independent parts, one for each index of `grp`. A program takes and returns all parts, laid end to end along the dimension named above; each array names one. Nothing has to cross between parts.
Inputs may be any that keep to these rules, and one draw needn't show every extreme that they name: Among the tiles of one device at most 2 have the same owner, and some owner has exactly 2.
All inputs are finite; a program needn't handle non-finite values.
Results may differ from a plain program's by a relative error of at most 0.003.
Values may be sent and summed in bfloat16 or wider, within the bound.
A program may use at most 64 MiB of HBM per device.

v0:
```python
import functools

import jax
import jax.numpy as jnp
from jax import lax
from jax.experimental import pallas as pl
from jax.experimental.pallas import tpu as pltpu
from jax.sharding import PartitionSpec as P

TSTEP = 32
BLOCK = 128
MESH_ID = pl.DeviceIdType.MESH
F32 = jnp.float32
BF16 = jnp.bfloat16


def body(
    rows,
    hist_hbm,
    kern_hbm,
    trow_hbm,
    tcnt_hbm,
    own_hbm,
    spl_hbm,
    mode_hbm,
    nodal_out,
    modal_out,
    hist_in,
    kern,
    trow,
    tcnt,
    own,
    spl,
    mode,
    hist_t,
    window,
    part,
    part_in,
    force,
    force_send,
    force_in,
    modal_send,
    modal_in,
    local_sem,
    kern_sem,
    hist_sem,
    part_sem,
    force_ssem,
    force_rsem,
    modal_ssem,
    modal_rsem,
):
    lag = lax.axis_index("lag")
    me = lax.axis_index("row")
    press = kern.shape[0]
    pairs = press // 2
    lags = kern.shape[2]
    blocks = lags // BLOCK
    hlen = hist_in.shape[1]
    half = TSTEP // 2

    hist_copy = pltpu.make_async_copy(hist_hbm, hist_in, local_sem.at[0])
    hist_copy.start()
    barrier = pltpu.get_barrier_semaphore()
    pl.semaphore_signal(barrier, inc=1, device_id={"lag": 1 - lag}, device_id_type=MESH_ID)
    for o in range(1, rows):
        pl.semaphore_signal(
            barrier, inc=1, device_id={"row": lax.rem(me + o, rows)}, device_id_type=MESH_ID
        )
    small = [
        pltpu.make_async_copy(src, dst, local_sem.at[1 + n])
        for n, (src, dst) in enumerate(
            [(trow_hbm, trow), (tcnt_hbm, tcnt), (own_hbm, own), (spl_hbm, spl), (mode_hbm, mode)]
        )
    ]

    def kern_copy(p):
        at = pl.ds(2 * p, 2)
        return pltpu.make_async_copy(kern_hbm.at[at], kern.at[at], kern_sem.at[p])

    for p in range(pairs):
        kern_copy(p).start()
    for copy in small:
        copy.start()

    hist_copy.wait()
    hist_t[...] = hist_in[...].T
    pl.semaphore_wait(barrier, rows)
    hist_send = pltpu.make_async_remote_copy(
        src_ref=hist_t,
        dst_ref=window.at[pl.ds(pl.multiple_of(half * lag, half), hlen)],
        send_sem=hist_sem.at[0],
        recv_sem=hist_sem.at[1],
        device_id={"lag": 1 - lag},
        device_id_type=MESH_ID,
    )
    hist_send.start()
    window[pl.ds(pl.multiple_of(hlen * lag, half), half), :] = hist_t[
        pl.ds(pl.multiple_of((hlen - half) * (1 - lag), half), half), :
    ]

    for copy in small:
        copy.wait()
    tiles, tp = trow.shape
    picks = tiles * tp
    e_lane = lax.broadcasted_iota(jnp.int32, (tp, picks), 1)
    e_row = lax.broadcasted_iota(jnp.int32, (tp, picks), 0)
    spread = (lax.rem(e_lane, tp) == e_row).astype(BF16)
    t_lane = lax.broadcasted_iota(jnp.int32, (tiles, picks), 1)
    t_row = lax.broadcasted_iota(jnp.int32, (tiles, picks), 0)
    mine = lax.div(t_lane, tp) == t_row
    row_at = jnp.dot(trow[...].astype(F32).astype(BF16), spread, preferred_element_type=F32)
    row_at = jnp.sum(jnp.where(mine, row_at, 0.0), axis=0, keepdims=True)
    own_at = jnp.sum(jnp.where(mine, own[...].astype(F32), 0.0), axis=0, keepdims=True)
    lane = lax.broadcasted_iota(jnp.int32, (1, picks), 1)
    tile_at = lax.div(lane, tp)
    count_at = jnp.zeros((1, picks), jnp.int32)
    for i in range(tiles):
        count_at = jnp.where(tile_at == i, tcnt[i], count_at)
    row_at = jnp.where(lax.rem(lane, tp) < count_at, row_at, -1.0)
    r_iota = lax.broadcasted_iota(jnp.int32, (BLOCK, picks), 0).astype(F32)
    picker = (r_iota == row_at).astype(F32).astype(BF16)

    hist_send.wait()

    b_lane = lax.broadcasted_iota(jnp.int32, (1, 2 * BLOCK), 1)
    shift = (BLOCK - 1) - lax.rem(b_lane, BLOCK)
    lane1 = lax.broadcasted_iota(jnp.int32, (TSTEP, BLOCK), 1)

    def pair(p, acc):
        kern_copy(p).wait()
        total = None
        for a in range(blocks):
            cols = slice(a * BLOCK, (a + 1) * BLOCK)
            w = jnp.concatenate([kern[2 * p, :, cols], kern[2 * p + 1, :, cols]], axis=1)
            start = lags - BLOCK * (a + 1)
            x = window[start : start + BLOCK + TSTEP, :]
            y = jnp.dot(x, w, preferred_element_type=F32)
            total = y if total is None else total + y
        bit, length = BLOCK // 2, BLOCK
        while bit >= 8:
            length = TSTEP + bit
            up = total[bit : bit + length]
            total = jnp.where((shift & bit) != 0, up, total[:length])
            bit //= 2
        for bit in (4, 2, 1):
            up = pltpu.roll(total, total.shape[0] - bit, 0)
            total = jnp.where((shift & bit) != 0, up, total)
        total = total[:TSTEP]
        s0 = jnp.sum(total[:, :BLOCK], axis=1, keepdims=True)
        s1 = jnp.sum(total[:, BLOCK:], axis=1, keepdims=True)
        acc = jnp.where(lane1 == 2 * p, s0, acc)
        return jnp.where(lane1 == 2 * p + 1, s1, acc)

    acc = lax.fori_loop(0, pairs, pair, jnp.zeros((TSTEP, BLOCK), F32))
    part[...] = acc.reshape(2, half, BLOCK)
    part_send = pltpu.make_async_remote_copy(
        src_ref=part.at[1 - lag],
        dst_ref=part_in,
        send_sem=part_sem.at[0],
        recv_sem=part_sem.at[1],
        device_id={"lag": 1 - lag},
        device_id_type=MESH_ID,
    )
    part_send.start()
    part_send.wait_recv()
    pressure = (part[lag] + part_in[...]).astype(BF16)

    tile_in = jnp.dot(pressure, picker, preferred_element_type=F32)
    owned = jnp.concatenate(
        [jnp.where(own_at == float(d), tile_in, 0.0) for d in range(rows)], axis=0
    ).astype(BF16)
    flat = jnp.dot(owned, spl[...].reshape(picks, spl.shape[2]), preferred_element_type=F32)
    force[...] = flat.reshape(rows, half, spl.shape[2])
    force_send[...] = force[...].astype(force_send.dtype)

    def exchange(sources, dest, ssem, rsem):
        copies = [
            pltpu.make_async_remote_copy(
                src_ref=sources(lax.rem(me + o, rows)),
                dst_ref=dest.at[o - 1],
                send_sem=ssem.at[o - 1],
                recv_sem=rsem.at[o - 1],
                device_id={"row": lax.rem(me + o, rows)},
                device_id_type=MESH_ID,
            )
            for o in range(1, rows)
        ]
        for copy in copies:
            copy.start()
        return copies

    force_copies = exchange(lambda d: force_send.at[d], force_in, force_ssem, force_rsem)
    nodal = force[me]
    for o, copy in enumerate(force_copies):
        copy.wait_recv()
        nodal = nodal + force_in[o].astype(F32)
    share = jnp.dot(
        nodal, mode[...], preferred_element_type=F32, precision=lax.Precision.HIGHEST
    )
    modal_send[...] = share.astype(modal_send.dtype)
    modal_copies = exchange(lambda d: modal_send, modal_in, modal_ssem, modal_rsem)
    nodal_out[...] = nodal
    for o, copy in enumerate(modal_copies):
        copy.wait_recv()
        share = share + modal_in[o].astype(F32)
    modal_out[...] = share
    part_send.wait_send()
    for copy in force_copies + modal_copies:
        copy.wait_send()


def on_device(history, kernel, tile_rows, tile_counts, owner, spline, mode_shapes):
    rows = lax.axis_size("row")
    modes, hlen = history.shape
    press, _, lags = kernel.shape
    tiles, tp = tile_rows.shape
    ndof = spline.shape[2]
    half = TSTEP // 2
    dma = pltpu.SemaphoreType.DMA
    return pl.pallas_call(
        functools.partial(body, rows),
        out_shape=(
            jax.ShapeDtypeStruct((half, ndof), F32),
            jax.ShapeDtypeStruct((half, modes), F32),
        ),
        in_specs=[pl.BlockSpec(memory_space=pl.ANY)] * 7,
        out_specs=(
            pl.BlockSpec(memory_space=pltpu.VMEM),
            pl.BlockSpec(memory_space=pltpu.VMEM),
        ),
        scratch_shapes=[
            pltpu.VMEM((modes, hlen), BF16),
            pltpu.VMEM((press, modes, lags), BF16),
            pltpu.VMEM((tiles, tp), jnp.int32),
            pltpu.SMEM((tiles,), jnp.int32),
            pltpu.VMEM((tiles, 1), jnp.int32),
            pltpu.VMEM(spline.shape, BF16),
            pltpu.VMEM(mode_shapes.shape, F32),
            pltpu.VMEM((hlen, modes), BF16),
            pltpu.VMEM((hlen + half, modes), BF16),
            pltpu.VMEM((2, half, BLOCK), F32),
            pltpu.VMEM((half, BLOCK), F32),
            pltpu.VMEM((rows, half, ndof), F32),
            pltpu.VMEM((rows, half, ndof), BF16),
            pltpu.VMEM((rows - 1, half, ndof), BF16),
            pltpu.VMEM((half, modes), BF16),
            pltpu.VMEM((rows - 1, half, modes), BF16),
            dma((6,)),
            dma((press // 2,)),
            dma((2,)),
            dma((2,)),
            dma((rows - 1,)),
            dma((rows - 1,)),
            dma((rows - 1,)),
            dma((rows - 1,)),
        ],
        compiler_params=pltpu.CompilerParams(
            collective_id=0, has_side_effects=True, vmem_limit_bytes=40 * 1024 * 1024
        ),
    )(history, kernel, tile_rows, tile_counts, owner, spline, mode_shapes)


def solution(mesh):
    return jax.shard_map(
        on_device,
        mesh=mesh,
        in_specs=(
            P("grp", "lag"),
            P(("grp", "row"), None, "lag"),
            P(("grp", "row"), None),
            P(("grp", "row")),
            P(("grp", "row"), None),
            P(("grp", "row"), None, None),
            P(("grp", "row"), None),
        ),
        out_specs=(P("lag", ("grp", "row")), P("lag", "grp")),
        check_vma=False,
    )
```

profile of v0, /device:TPU:0, one launch (start us, length us, event | category | flops | bytes accessed | tf_op | source)
XLA Modules:
  0.0 31.1 jit_solution(17159388217167510351)
XLA Ops:
  0.6 0.7 %copy.9.own_hbm = s32[8,1]{1,0:T(8,128)S(1)} copy(s32[8,1]{0,1:T(1,128)} %param.11) | data formatting | bytes 64 | tf_op args[4]
  1.4 1.0 %copy.10.mode_hbm = f32[128,200]{1,0:T(8,128)S(1)} copy(f32[128,200]{0,1:T(8,128)} %param.13) | data formatting | bytes 204800 | tf_op args[6]
  2.4 0.0 copy-start
  2.4 2.9 %copy-done = bf16[16,200,1024]{2,1,0:T(8,128)(2,1)S(1)} copy-done((bf16[16,200,1024]{2,1,0:T(8,128)(2,1)S(1)}, bf16[16,200,1024]{2,1,0:T(8,128)(2,1)}, u32[]{:S(2)}) %copy-start) | copy-done | bytes 6553624
  5.2 0.0 copy-start.1
  5.2 1.0 %copy-done.1 = bf16[200,1040]{1,0:T(8,128)(2,1)S(1)} copy-done((bf16[200,1040]{1,0:T(8,128)(2,1)S(1)}, bf16[200,1040]{1,0:T(8,128)(2,1)}, u32[]{:S(2)}) %copy-start.1) | copy-done | bytes 416024
  6.2 0.0 copy-start.2
  6.2 0.8 %copy-done.2 = bf16[8,16,128]{2,1,0:T(8,128)(2,1)S(1)} copy-done((bf16[8,16,128]{2,1,0:T(8,128)(2,1)S(1)}, bf16[8,16,128]{2,1,0:T(8,128)(2,1)}, u32[]{:S(2)}) %copy-start.2) | copy-done | bytes 32792
  7.0 0.0 copy-start.3
  7.0 0.7 %copy-done.3 = s32[8,16]{1,0:T(8,128)S(1)} copy-done((s32[8,16]{1,0:T(8,128)S(1)}, s32[8,16]{1,0:T(8,128)}, u32[]{:S(2)}) %copy-start.3) | copy-done | bytes 536
  7.7 0.0 copy-start.4
  7.7 0.7 %copy-done.4 = s32[8]{0:T(128)S(1)} copy-done((s32[8]{0:T(128)S(1)}, s32[8]{0:T(128)}, u32[]{:S(2)}) %copy-start.4) | copy-done | bytes 56
  8.3 21.5 %shard_map.86 = (f32[16,128]{1,0:T(8,128)S(1)}, f32[16,200]{1,0:T(8,128)S(1)}) custom-call(bf16[200,1040]{1,0:T(8,128)(2,1)S(1)} %copy-done.1, bf16[16,200,1024]{2,1,0:T(8,128)(2,1)S(1)} %copy-done, s32[8,16]{1,0:T(8,128)S(1)} %copy-done.3, s32[8]{0:T(128)S(1)} %copy-done.4, s32[8,1]{1,0:T(8,128)S(1)} %copy.9.own_hbm, bf16[8,16,128]{2,1,0:T(8,128)(2,1)S(1)} %copy-done.2, ...), custom_call_target="tpu_custom_call" | custom-call | tf_op jit(solution)/shard_map/pallas_call | solution.py:221
  29.9 0.6 %copy.13 = f32[16,128]{1,0:T(8,128)} copy(f32[16,128]{1,0:T(8,128)S(1)} %get-tuple-element.4) | data formatting | bytes 16384
  30.5 0.6 %copy.14 = f32[16,200]{1,0:T(8,128)} copy(f32[16,200]{1,0:T(8,128)S(1)} %get-tuple-element.5) | data formatting | bytes 25600
Async XLA Ops:
  2.4 2.9 %copy-start = (bf16[16,200,1024]{2,1,0:T(8,128)(2,1)S(1)}, bf16[16,200,1024]{2,1,0:T(8,128)(2,1)}, u32[]{:S(2)}) copy-start(bf16[16,200,1024]{2,1,0:T(8,128)(2,1)} %kern_hbm.1) | copy-start | bytes 19660804
  5.2 1.0 %copy-start.1 = (bf16[200,1040]{1,0:T(8,128)(2,1)S(1)}, bf16[200,1040]{1,0:T(8,128)(2,1)}, u32[]{:S(2)}) copy-start(bf16[200,1040]{1,0:T(8,128)(2,1)} %hist_hbm.1) | copy-start | bytes 1248004
  6.2 0.8 %copy-start.2 = (bf16[8,16,128]{2,1,0:T(8,128)(2,1)S(1)}, bf16[8,16,128]{2,1,0:T(8,128)(2,1)}, u32[]{:S(2)}) copy-start(bf16[8,16,128]{2,1,0:T(8,128)(2,1)} %spl_hbm.1) | copy-start | bytes 98308
  7.0 0.7 %copy-start.3 = (s32[8,16]{1,0:T(8,128)S(1)}, s32[8,16]{1,0:T(8,128)}, u32[]{:S(2)}) copy-start(s32[8,16]{1,0:T(8,128)} %trow_hbm.1) | copy-start | bytes 1540
  7.7 0.7 %copy-start.4 = (s32[8]{0:T(128)S(1)}, s32[8]{0:T(128)}, u32[]{:S(2)}) copy-start(s32[8]{0:T(128)} %tcnt_hbm.1) | copy-start | bytes 100
where the time goes:
time: 31.4 us; the launch traced here: 31.1 us
  Pallas kernels  21.5 us (68%)
  local copies, waits for them, and re-layouts  8.9 us (28%)
  between operations  0.66 us (2%)
    pallas_call x1, Pallas kernels, on_device(): pl.pallas_call(functools.partial(body, rows), out_shape=(jax.ShapeDtypeSt...  21.5 us
    unnamed x14, local copies, waits for them, and re-layouts  8.9 us

commit v1 on v0

--- a/solution.py
+++ b/solution.py
@@ -37,7 +37,6 @@
     part,
     part_in,
     force,
-    force_send,
     force_in,
     modal_send,
     modal_in,
@@ -111,12 +110,13 @@
     mine = lax.div(t_lane, tp) == t_row
     row_at = jnp.dot(trow[...].astype(F32).astype(BF16), spread, preferred_element_type=F32)
     row_at = jnp.sum(jnp.where(mine, row_at, 0.0), axis=0, keepdims=True)
-    own_at = jnp.sum(jnp.where(mine, own[...].astype(F32), 0.0), axis=0, keepdims=True)
     lane = lax.broadcasted_iota(jnp.int32, (1, picks), 1)
     tile_at = lax.div(lane, tp)
     count_at = jnp.zeros((1, picks), jnp.int32)
+    own_at = jnp.zeros((1, picks), jnp.int32)
     for i in range(tiles):
         count_at = jnp.where(tile_at == i, tcnt[i], count_at)
+        own_at = jnp.where(tile_at == i, own[i], own_at)
     row_at = jnp.where(lax.rem(lane, tp) < count_at, row_at, -1.0)
     r_iota = lax.broadcasted_iota(jnp.int32, (BLOCK, picks), 0).astype(F32)
     picker = (r_iota == row_at).astype(F32).astype(BF16)
@@ -168,11 +168,10 @@
 
     tile_in = jnp.dot(pressure, picker, preferred_element_type=F32)
     owned = jnp.concatenate(
-        [jnp.where(own_at == float(d), tile_in, 0.0) for d in range(rows)], axis=0
+        [jnp.where(own_at == d, tile_in, 0.0) for d in range(rows)], axis=0
     ).astype(BF16)
     flat = jnp.dot(owned, spl[...].reshape(picks, spl.shape[2]), preferred_element_type=F32)
     force[...] = flat.reshape(rows, half, spl.shape[2])
-    force_send[...] = force[...].astype(force_send.dtype)
 
     def exchange(sources, dest, ssem, rsem):
         copies = [
@@ -190,13 +189,17 @@
             copy.start()
         return copies
 
-    force_copies = exchange(lambda d: force_send.at[d], force_in, force_ssem, force_rsem)
+    force_copies = exchange(lambda d: force.at[d], force_in, force_ssem, force_rsem)
     nodal = force[me]
     for o, copy in enumerate(force_copies):
         copy.wait_recv()
         nodal = nodal + force_in[o].astype(F32)
-    share = jnp.dot(
-        nodal, mode[...], preferred_element_type=F32, precision=lax.Precision.HIGHEST
+    share = lax.dot_general(
+        nodal,
+        mode[...],
+        (((1,), (1,)), ((), ())),
+        preferred_element_type=F32,
+        precision=lax.Precision.HIGHEST,
     )
     modal_send[...] = share.astype(modal_send.dtype)
     modal_copies = exchange(lambda d: modal_send, modal_in, modal_ssem, modal_rsem)
@@ -234,16 +237,15 @@
             pltpu.VMEM((press, modes, lags), BF16),
             pltpu.VMEM((tiles, tp), jnp.int32),
             pltpu.SMEM((tiles,), jnp.int32),
-            pltpu.VMEM((tiles, 1), jnp.int32),
+            pltpu.SMEM((tiles,), jnp.int32),
             pltpu.VMEM(spline.shape, BF16),
-            pltpu.VMEM(mode_shapes.shape, F32),
+            pltpu.VMEM((modes, ndof), F32),
             pltpu.VMEM((hlen, modes), BF16),
             pltpu.VMEM((hlen + half, modes), BF16),
             pltpu.VMEM((2, half, BLOCK), F32),
             pltpu.VMEM((half, BLOCK), F32),
             pltpu.VMEM((rows, half, ndof), F32),
-            pltpu.VMEM((rows, half, ndof), BF16),
-            pltpu.VMEM((rows - 1, half, ndof), BF16),
+            pltpu.VMEM((rows - 1, half, ndof), F32),
             pltpu.VMEM((half, modes), BF16),
             pltpu.VMEM((rows - 1, half, modes), BF16),
             dma((6,)),
@@ -256,9 +258,9 @@
             dma((rows - 1,)),
         ],
         compiler_params=pltpu.CompilerParams(
-            collective_id=0, has_side_effects=True, vmem_limit_bytes=40 * 1024 * 1024
-        ),
-    )(history, kernel, tile_rows, tile_counts, owner, spline, mode_shapes)
+            collective_id=0, has_side_effects=True, vmem_limit_bytes=60 * 1024 * 1024
+        ),
+    )(history, kernel, tile_rows, tile_counts, owner.reshape(tiles), spline, mode_shapes.T)
 
 
 def solution(mesh):

time: 31.4 us -> 25.8 us (0.82)
  local copies, waits for them, and re-layouts: 8.9 us -> 2.62 us
  Pallas kernels: 21.5 us -> 22.2 us
    unnamed x14 -> x2, local copies, waits for them, and re-layouts: 8.9 us -> 2.62 us
    pallas_call x1, Pallas kernels: 21.5 us -> 22.2 us  [on_device(): pl.pallas_call(functools.partial(body, rows), out_shape=(jax.ShapeDtypeSt...]
where the time goes in v1:
time: 25.8 us; the launch traced here: 25.5 us
  Pallas kernels  22.2 us (86%)
  local copies, waits for them, and re-layouts  2.62 us (10%)
  between operations  0.64 us (2%)
    pallas_call x1, Pallas kernels, on_device(): pl.pallas_call(functools.partial(body, rows), out_shape=(jax.ShapeDtypeSt...  22.2 us
    unnamed x2, local copies, waits for them, and re-layouts  2.62 us

profile of v1, /device:TPU:0, one launch (start us, length us, event | category | flops | bytes accessed | tf_op | source)
XLA Modules:
  0.0 25.5 jit_solution(316798028554101341)
XLA Ops:
  0.6 22.2 %shard_map.86 = (f32[16,128]{1,0:T(8,128)}, f32[16,200]{1,0:T(8,128)}) custom-call(bf16[200,1040]{1,0:T(8,128)(2,1)} %hist_hbm.1, bf16[16,200,1024]{2,1,0:T(8,128)(2,1)} %kern_hbm.1, s32[8,16]{1,0:T(8,128)} %trow_hbm.1, s32[8]{0:T(128)} %tcnt_hbm.1, s32[8]{0:T(128)} %bitcast.3, bf16[8,16,128]{2,1,0:T(8,128)(2,1)} %spl_hbm.1, f32[200,128]{1,0:T(8,128)} %bitcast.2), custom_call_target="tpu_custom_call" | custom-call | tf_op jit(solution)/shard_map/pallas_call | solution.py:224
  22.9 1.3 %copy.11 = f32[16,128]{1,0:T(8,128)} copy(f32[16,128]{1,0:T(8,128)} %get-tuple-element.4) | data formatting | bytes 16384
  24.2 1.3 %copy.12 = f32[16,200]{1,0:T(8,128)} copy(f32[16,200]{1,0:T(8,128)} %get-tuple-element.5) | data formatting | bytes 25600

commit v2 on v1

--- a/solution.py
+++ b/solution.py
@@ -32,6 +32,7 @@
     own,
     spl,
     mode,
+    mode_split,
     hist_t,
     window,
     part,
@@ -83,17 +84,23 @@
         copy.start()
 
     hist_copy.wait()
-    hist_t[...] = hist_in[...].T
-    pl.semaphore_wait(barrier, rows)
-    hist_send = pltpu.make_async_remote_copy(
-        src_ref=hist_t,
-        dst_ref=window.at[pl.ds(pl.multiple_of(half * lag, half), hlen)],
-        send_sem=hist_sem.at[0],
-        recv_sem=hist_sem.at[1],
-        device_id={"lag": 1 - lag},
-        device_id_type=MESH_ID,
-    )
-    hist_send.start()
+    cuts = [0, 2 * BLOCK, 4 * BLOCK, 6 * BLOCK, hlen]
+    hist_sends = []
+    for n in range(4):
+        lo, size = cuts[n], cuts[n + 1] - cuts[n]
+        hist_t[lo : lo + size, :] = hist_in[:, lo : lo + size].T
+        if n == 0:
+            pl.semaphore_wait(barrier, rows)
+        send = pltpu.make_async_remote_copy(
+            src_ref=hist_t.at[pl.ds(lo, size)],
+            dst_ref=window.at[pl.ds(pl.multiple_of(half * lag + lo, half), size)],
+            send_sem=hist_sem.at[n],
+            recv_sem=hist_sem.at[4 + n],
+            device_id={"lag": 1 - lag},
+            device_id_type=MESH_ID,
+        )
+        send.start()
+        hist_sends.append(send)
     window[pl.ds(pl.multiple_of(hlen * lag, half), half), :] = hist_t[
         pl.ds(pl.multiple_of((hlen - half) * (1 - lag), half), half), :
     ]
@@ -121,14 +128,24 @@
     r_iota = lax.broadcasted_iota(jnp.int32, (BLOCK, picks), 0).astype(F32)
     picker = (r_iota == row_at).astype(F32).astype(BF16)
 
-    hist_send.wait()
+    modes_t = mode[...].T
+    mode_hi = modes_t.astype(BF16)
+    mode_lo = (modes_t - mode_hi.astype(F32)).astype(BF16)
+    ndof = modes_t.shape[0]
+    mode_split[0:ndof, :] = mode_hi
+    mode_split[ndof : 2 * ndof, :] = mode_lo
+    mode_split[2 * ndof : 3 * ndof, :] = mode_hi
+
+    for p in range(pairs):
+        kern_copy(p).wait()
+    for send in hist_sends:
+        send.wait()
 
     b_lane = lax.broadcasted_iota(jnp.int32, (1, 2 * BLOCK), 1)
     shift = (BLOCK - 1) - lax.rem(b_lane, BLOCK)
     lane1 = lax.broadcasted_iota(jnp.int32, (TSTEP, BLOCK), 1)
 
     def pair(p, acc):
-        kern_copy(p).wait()
         total = None
         for a in range(blocks):
             cols = slice(a * BLOCK, (a + 1) * BLOCK)
@@ -152,7 +169,7 @@
         acc = jnp.where(lane1 == 2 * p, s0, acc)
         return jnp.where(lane1 == 2 * p + 1, s1, acc)
 
-    acc = lax.fori_loop(0, pairs, pair, jnp.zeros((TSTEP, BLOCK), F32))
+    acc = lax.fori_loop(0, pairs, pair, jnp.zeros((TSTEP, BLOCK), F32), unroll=2)
     part[...] = acc.reshape(2, half, BLOCK)
     part_send = pltpu.make_async_remote_copy(
         src_ref=part.at[1 - lag],
@@ -194,12 +211,12 @@
     for o, copy in enumerate(force_copies):
         copy.wait_recv()
         nodal = nodal + force_in[o].astype(F32)
-    share = lax.dot_general(
-        nodal,
-        mode[...],
-        (((1,), (1,)), ((), ())),
+    nodal_hi = nodal.astype(BF16)
+    nodal_lo = (nodal - nodal_hi.astype(F32)).astype(BF16)
+    share = jnp.dot(
+        jnp.concatenate([nodal_hi, nodal_hi, nodal_lo], axis=1),
+        mode_split[...],
         preferred_element_type=F32,
-        precision=lax.Precision.HIGHEST,
     )
     modal_send[...] = share.astype(modal_send.dtype)
     modal_copies = exchange(lambda d: modal_send, modal_in, modal_ssem, modal_rsem)
@@ -224,10 +241,10 @@
     return pl.pallas_call(
         functools.partial(body, rows),
         out_shape=(
-            jax.ShapeDtypeStruct((half, ndof), F32),
-            jax.ShapeDtypeStruct((half, modes), F32),
-        ),
-        in_specs=[pl.BlockSpec(memory_space=pl.ANY)] * 7,
+            pltpu.VMEM((half, ndof), F32),
+            pltpu.VMEM((half, modes), F32),
+        ),
+        in_specs=[pl.BlockSpec(memory_space=pltpu.HBM)] * 7,
         out_specs=(
             pl.BlockSpec(memory_space=pltpu.VMEM),
             pl.BlockSpec(memory_space=pltpu.VMEM),
@@ -240,6 +257,7 @@
             pltpu.SMEM((tiles,), jnp.int32),
             pltpu.VMEM(spline.shape, BF16),
             pltpu.VMEM((modes, ndof), F32),
+            pltpu.VMEM((3 * ndof, modes), BF16),
             pltpu.VMEM((hlen, modes), BF16),
             pltpu.VMEM((hlen + half, modes), BF16),
             pltpu.VMEM((2, half, BLOCK), F32),
@@ -250,7 +268,7 @@
             pltpu.VMEM((rows - 1, half, modes), BF16),
             dma((6,)),
             dma((press // 2,)),
-            dma((2,)),
+            dma((8,)),
             dma((2,)),
             dma((rows - 1,)),
             dma((rows - 1,)),
@@ -258,7 +276,7 @@
             dma((rows - 1,)),
         ],
         compiler_params=pltpu.CompilerParams(
-            collective_id=0, has_side_effects=True, vmem_limit_bytes=60 * 1024 * 1024
+            collective_id=0, has_side_effects=True, vmem_limit_bytes=61440 * 1024
         ),
     )(history, kernel, tile_rows, tile_counts, owner.reshape(tiles), spline, mode_shapes.T)
 

time: 25.8 us -> 22.8 us (0.88)
  local copies, waits for them, and re-layouts: 2.62 us -> 1.21 us
  Pallas kernels: 22.2 us -> 20.8 us
    pallas_call x1, Pallas kernels: 22.2 us -> 20.8 us  [on_device(): pl.pallas_call(functools.partial(body, rows), out_shape=(pltpu.VMEM((half...]
    unnamed x2, local copies, waits for them, and re-layouts: 2.62 us -> 1.21 us
where the time goes in v2:
time: 22.8 us; the launch traced here: 22.6 us
  Pallas kernels  20.8 us (91%)
  local copies, waits for them, and re-layouts  1.21 us (5%)
  between operations  0.64 us (3%)
    pallas_call x1, Pallas kernels, on_device(): pl.pallas_call(functools.partial(body, rows), out_shape=(pltpu.VMEM((half...  20.8 us
    unnamed x2, local copies, waits for them, and re-layouts  1.21 us

profile of v2, /device:TPU:0, one launch (start us, length us, event | category | flops | bytes accessed | tf_op | source)
XLA Modules:
  0.0 22.6 jit_solution(9303265839781183479)
XLA Ops:
  0.6 20.8 %shard_map.86 = (f32[16,128]{1,0:T(8,128)S(1)}, f32[16,200]{1,0:T(8,128)S(1)}) custom-call(bf16[200,1040]{1,0:T(8,128)(2,1)} %hist_hbm.1, bf16[16,200,1024]{2,1,0:T(8,128)(2,1)} %kern_hbm.1, s32[8,16]{1,0:T(8,128)} %trow_hbm.1, s32[8]{0:T(128)} %tcnt_hbm.1, s32[8]{0:T(128)} %bitcast.3, bf16[8,16,128]{2,1,0:T(8,128)(2,1)} %spl_hbm.1, f32[200,128]{1,0:T(8,128)} %bitcast.2), custom_call_target="tpu_custom_call" | custom-call | tf_op jit(solution)/shard_map/pallas_call | solution.py:241
  21.4 0.6 %copy.11 = f32[16,128]{1,0:T(8,128)} copy(f32[16,128]{1,0:T(8,128)S(1)} %get-tuple-element.2) | data formatting | bytes 16384
  22.0 0.6 %copy.12 = f32[16,200]{1,0:T(8,128)} copy(f32[16,200]{1,0:T(8,128)S(1)} %get-tuple-element.3) | data formatting | bytes 25600

commit v3 on v2

--- a/solution.py
+++ b/solution.py
@@ -59,8 +59,16 @@
     hlen = hist_in.shape[1]
     half = TSTEP // 2
 
-    hist_copy = pltpu.make_async_copy(hist_hbm, hist_in, local_sem.at[0])
-    hist_copy.start()
+    cuts = [0, 2 * BLOCK, 4 * BLOCK, 6 * BLOCK, hlen]
+    spans = [(cuts[n], cuts[n + 1] - cuts[n]) for n in range(4)]
+    hist_copies = [
+        pltpu.make_async_copy(
+            hist_hbm.at[:, pl.ds(lo, size)], hist_in.at[:, pl.ds(lo, size)], local_sem.at[6 + n]
+        )
+        for n, (lo, size) in enumerate(spans)
+    ]
+    for copy in hist_copies:
+        copy.start()
     barrier = pltpu.get_barrier_semaphore()
     pl.semaphore_signal(barrier, inc=1, device_id={"lag": 1 - lag}, device_id_type=MESH_ID)
     for o in range(1, rows):
@@ -83,11 +91,9 @@
     for copy in small:
         copy.start()
 
-    hist_copy.wait()
-    cuts = [0, 2 * BLOCK, 4 * BLOCK, 6 * BLOCK, hlen]
     hist_sends = []
-    for n in range(4):
-        lo, size = cuts[n], cuts[n + 1] - cuts[n]
+    for n, (lo, size) in enumerate(spans):
+        hist_copies[n].wait()
         hist_t[lo : lo + size, :] = hist_in[:, lo : lo + size].T
         if n == 0:
             pl.semaphore_wait(barrier, rows)
@@ -169,7 +175,7 @@
         acc = jnp.where(lane1 == 2 * p, s0, acc)
         return jnp.where(lane1 == 2 * p + 1, s1, acc)
 
-    acc = lax.fori_loop(0, pairs, pair, jnp.zeros((TSTEP, BLOCK), F32), unroll=2)
+    acc = lax.fori_loop(0, pairs, pair, jnp.zeros((TSTEP, BLOCK), F32), unroll=4)
     part[...] = acc.reshape(2, half, BLOCK)
     part_send = pltpu.make_async_remote_copy(
         src_ref=part.at[1 - lag],
@@ -230,6 +236,17 @@
         copy.wait_send()
 
 
+def write_out(nodal, modal, nodal_out, modal_out, sem):
+    copies = [
+        pltpu.make_async_copy(nodal, nodal_out, sem.at[0]),
+        pltpu.make_async_copy(modal, modal_out, sem.at[1]),
+    ]
+    for copy in copies:
+        copy.start()
+    for copy in copies:
+        copy.wait()
+
+
 def on_device(history, kernel, tile_rows, tile_counts, owner, spline, mode_shapes):
     rows = lax.axis_size("row")
     modes, hlen = history.shape
@@ -238,7 +255,7 @@
     ndof = spline.shape[2]
     half = TSTEP // 2
     dma = pltpu.SemaphoreType.DMA
-    return pl.pallas_call(
+    nodal, modal = pl.pallas_call(
         functools.partial(body, rows),
         out_shape=(
             pltpu.VMEM((half, ndof), F32),
@@ -266,7 +283,7 @@
             pltpu.VMEM((rows - 1, half, ndof), F32),
             pltpu.VMEM((half, modes), BF16),
             pltpu.VMEM((rows - 1, half, modes), BF16),
-            dma((6,)),
+            dma((10,)),
             dma((press // 2,)),
             dma((8,)),
             dma((2,)),
@@ -279,6 +296,14 @@
             collective_id=0, has_side_effects=True, vmem_limit_bytes=61440 * 1024
         ),
     )(history, kernel, tile_rows, tile_counts, owner.reshape(tiles), spline, mode_shapes.T)
+    return pl.pallas_call(
+        write_out,
+        out_shape=(pltpu.HBM((half, ndof), F32), pltpu.HBM((half, modes), F32)),
+        in_specs=[pl.BlockSpec(memory_space=pltpu.VMEM)] * 2,
+        out_specs=(pl.BlockSpec(memory_space=pltpu.HBM), pl.BlockSpec(memory_space=pltpu.HBM)),
+        scratch_shapes=[dma((2,))],
+        compiler_params=pltpu.CompilerParams(vmem_limit_bytes=1024 * 1024),
+    )(nodal, modal)
 
 
 def solution(mesh):

time: 22.8 us -> 21.8 us (0.956)
  local copies, waits for them, and re-layouts: 1.21 us -> 0 us
    unnamed x2 -> x0, local copies, waits for them, and re-layouts: 1.21 us -> none
    pallas_call x0 -> x1, Pallas kernels: none -> 0.63 us  [on_device(): pl.pallas_call(write_out, out_shape=(pltpu.HBM((half, ndof), F32), pltpu....]
    pallas_call x1, Pallas kernels: 20.8 us -> 20.4 us  [on_device(): pl.pallas_call(functools.partial(body, rows), out_shape=(pltpu.VMEM((half...]
where the time goes in v3:
time: 21.8 us; the launch traced here: 21.7 us
  Pallas kernels  21 us (96%)
  between operations  0.64 us (3%)
    pallas_call x1, Pallas kernels, on_device(): pl.pallas_call(functools.partial(body, rows), out_shape=(pltpu.VMEM((half...  20.4 us
    pallas_call x1, Pallas kernels, on_device(): pl.pallas_call(write_out, out_shape=(pltpu.HBM((half, ndof), F32), pltpu....  0.63 us

profile of v3, /device:TPU:0, one launch (start us, length us, event | category | flops | bytes accessed | tf_op | source)
XLA Modules:
  0.0 21.7 jit_solution(395926124721103684)
XLA Ops:
  0.6 20.4 %shard_map.86 = (f32[16,128]{1,0:T(8,128)S(1)}, f32[16,200]{1,0:T(8,128)S(1)}) custom-call(bf16[200,1040]{1,0:T(8,128)(2,1)} %hist_hbm.1, bf16[16,200,1024]{2,1,0:T(8,128)(2,1)} %kern_hbm.1, s32[8,16]{1,0:T(8,128)} %trow_hbm.1, s32[8]{0:T(128)} %tcnt_hbm.1, s32[8]{0:T(128)} %bitcast.3, bf16[8,16,128]{2,1,0:T(8,128)(2,1)} %spl_hbm.1, f32[200,128]{1,0:T(8,128)} %bitcast.2), custom_call_target="tpu_custom_call" | custom-call | tf_op jit(solution)/shard_map/pallas_call | solution.py:258
  21.0 0.6 %shard_map.87 = (f32[16,128]{1,0:T(8,128)}, f32[16,200]{1,0:T(8,128)}) custom-call(f32[16,128]{1,0:T(8,128)S(1)} %get-tuple-element.4.nodal, f32[16,200]{1,0:T(8,128)S(1)} %get-tuple-element.5.modal), custom_call_target="tpu_custom_call" | custom-call | tf_op jit(solution)/shard_map/pallas_call | solution.py:299

commit v4 on v3

--- a/solution.py
+++ b/solution.py
@@ -175,7 +175,7 @@
         acc = jnp.where(lane1 == 2 * p, s0, acc)
         return jnp.where(lane1 == 2 * p + 1, s1, acc)
 
-    acc = lax.fori_loop(0, pairs, pair, jnp.zeros((TSTEP, BLOCK), F32), unroll=4)
+    acc = lax.fori_loop(0, pairs, pair, jnp.zeros((TSTEP, BLOCK), F32), unroll=8)
     part[...] = acc.reshape(2, half, BLOCK)
     part_send = pltpu.make_async_remote_copy(
         src_ref=part.at[1 - lag],

time: 21.8 us -> 21.5 us (0.986)
  Pallas kernels: 21 us -> 20.7 us
    pallas_call x1, Pallas kernels: 20.4 us -> 20.1 us  [on_device(): pl.pallas_call(functools.partial(body, rows), out_shape=(pltpu.VMEM((half...]
where the time goes in v4:
time: 21.5 us; the launch traced here: 21.4 us
  Pallas kernels  20.7 us (96%)
  between operations  0.64 us (3%)
    pallas_call x1, Pallas kernels, on_device(): pl.pallas_call(functools.partial(body, rows), out_shape=(pltpu.VMEM((half...  20.1 us
    pallas_call x1, Pallas kernels, on_device(): pl.pallas_call(write_out, out_shape=(pltpu.HBM((half, ndof), F32), pltpu....  0.63 us

profile of v4, /device:TPU:0, one launch (start us, length us, event | category | flops | bytes accessed | tf_op | source)
XLA Modules:
  0.0 21.4 jit_solution(13178382838246325459)
XLA Ops:
  0.6 20.1 %shard_map.86 = (f32[16,128]{1,0:T(8,128)S(1)}, f32[16,200]{1,0:T(8,128)S(1)}) custom-call(bf16[200,1040]{1,0:T(8,128)(2,1)} %hist_hbm.1, bf16[16,200,1024]{2,1,0:T(8,128)(2,1)} %kern_hbm.1, s32[8,16]{1,0:T(8,128)} %trow_hbm.1, s32[8]{0:T(128)} %tcnt_hbm.1, s32[8]{0:T(128)} %bitcast.3, bf16[8,16,128]{2,1,0:T(8,128)(2,1)} %spl_hbm.1, f32[200,128]{1,0:T(8,128)} %bitcast.2), custom_call_target="tpu_custom_call" | custom-call | tf_op jit(solution)/shard_map/pallas_call | solution.py:258
  20.7 0.6 %shard_map.87 = (f32[16,128]{1,0:T(8,128)}, f32[16,200]{1,0:T(8,128)}) custom-call(f32[16,128]{1,0:T(8,128)S(1)} %get-tuple-element.4.nodal, f32[16,200]{1,0:T(8,128)S(1)} %get-tuple-element.5.modal), custom_call_target="tpu_custom_call" | custom-call | tf_op jit(solution)/shard_map/pallas_call | solution.py:299
